TPU v7x, 512 devices: a whole 4x4x16 slice. The times are simulated.
512 devices in a mesh: sim: 32 (over z_lo, y, core), grp: 4 (over z_hi), gz: 4 (over x).
Axes of the slice: x: 4, y: 4, z: 16 (z_hi: 4, z_lo: 4; z = z_hi * 4 + z_lo), core: 2. Of those that a mesh axis runs over, the one named last changes fastest.
Arguments:
- fields: float32 [8, 2, 1024, 1024], P(None, None, 'sim', ('grp', 'gz')), may hold values from -6 to 6
- diffusivity: float32 [8], replicated, may hold values from 0.03 to 0.12
- velocity: float32 [2, 8], replicated, may hold values from -0.4 to 0.4
- coupling: float32 [8, 8], replicated, may hold values from -0.6 to 0.6
- basis_x: bfloat16 [1024, 128], replicated, may hold values from -0.1875 to 0.1875
- basis_y: bfloat16 [1024, 128], replicated, may hold values from -0.1875 to 0.1875
Outputs:
- fields_out: float32 [8, 2, 1024, 1024], P(None, None, 'sim', ('grp', 'gz'))
- gram_x: float32 [1024, 1024], P('sim', ('grp', 'gz'))
- gram_y: float32 [1024, 1024], P(('grp', 'gz'), 'sim')
- core: float32 [8, 2, 128, 128], P(None, None, 'sim', ('grp', 'gz'))
All inputs are finite; a program needn't handle non-finite values.
Results may differ from a plain program's by a relative error of at most 0.0003.
Values sent between devices are 32-bit elements; how exact they have to be, the bound alone decides.
A program may use at most 64 MiB of HBM per device.

v0:
```python
import jax
import jax.numpy as jnp
from jax import lax
from jax.sharding import PartitionSpec as P

NY = 1024
RANK = 128
STEPS = 2
time_step = 1.0
highest = lax.Precision.HIGHEST


def with_halo(cells, sides, width):
    for axis, dim in sides:
        count = lax.axis_size(axis)
        head = lax.slice_in_dim(cells, 0, width, axis=dim)
        tail = lax.slice_in_dim(cells, cells.shape[dim] - width, cells.shape[dim], axis=dim)
        cells = jnp.concatenate(
            [
                lax.ppermute(tail, axis, [(i, (i + 1) % count) for i in range(count)]),
                cells,
                lax.ppermute(head, axis, [((i + 1) % count, i) for i in range(count)]),
            ],
            axis=dim,
        )
    return cells


def rates(state, diffusivity, velocity, coupling):
    padded = with_halo(state, (("sim", 2), (("grp", "gz"), 3)), 1)
    center = padded[:, :, 1:-1, 1:-1]
    x_plus = padded[:, :, 2:, 1:-1]
    x_minus = padded[:, :, :-2, 1:-1]
    y_plus = padded[:, :, 1:-1, 2:]
    y_minus = padded[:, :, 1:-1, :-2]
    z_plus = jnp.roll(center, -1, 1)
    z_minus = jnp.roll(center, 1, 1)
    lapl = -6.0 * center + z_plus + z_minus + x_plus + x_minus + y_plus + y_minus
    grad_x = (x_plus - x_minus) * 0.5
    grad_y = (y_plus - y_minus) * 0.5
    react = jnp.einsum("fg,gzxy->fzxy", coupling, jnp.tanh(center), precision=highest)
    return (
        diffusivity[:, None, None, None] * lapl
        - velocity[0][:, None, None, None] * grad_x
        - velocity[1][:, None, None, None] * grad_y
        + react
    )


def shards(fields, diffusivity, velocity, coupling, basis_x, basis_y):
    state = fields
    for repeat in range(STEPS):
        first = rates(state, diffusivity, velocity, coupling)
        second = rates(state + 0.5 * time_step * first, diffusivity, velocity, coupling)
        third = rates(state + 0.5 * time_step * second, diffusivity, velocity, coupling)
        fourth = rates(state + time_step * third, diffusivity, velocity, coupling)
        state = state + time_step / 6.0 * (first + 2.0 * second + 2.0 * third + fourth)
    nfield = state.shape[0]
    depth = state.shape[1]
    x_rows = state.shape[2]
    y_cols = state.shape[3]
    basis_xf = basis_x.astype(jnp.float32)
    basis_yf = basis_y.astype(jnp.float32)
    block = jnp.einsum(
        "fzxy,fzwy->xw", state, lax.all_gather(state, "sim", axis=2, tiled=True), precision=highest
    )
    gram_rows = block
    own_basis = lax.dynamic_slice_in_dim(basis_xf, lax.axis_index("sim") * x_rows, x_rows, 0)
    partial_proj = jnp.einsum("xr,fzxy->fzry", own_basis, state, precision=highest)
    projected = lax.psum_scatter(partial_proj, "sim", scatter_dimension=2, tiled=True)
    gram_x = lax.psum_scatter(gram_rows, ("grp", "gz"), scatter_dimension=1, tiled=True) / (
        nfield * depth * NY
    )
    block = jnp.einsum(
        "fzry,fzrv->yv",
        projected,
        lax.all_gather(projected, ("grp", "gz"), axis=3, tiled=True),
        precision=highest,
    )
    own_basis_y = lax.dynamic_slice_in_dim(
        basis_yf, lax.axis_index(("grp", "gz")) * y_cols, y_cols, 0
    )
    partial_core = jnp.einsum("ys,fzry->fzrs", own_basis_y, projected, precision=highest)
    core = lax.psum_scatter(partial_core, ("grp", "gz"), scatter_dimension=3, tiled=True)
    gram_y = lax.psum_scatter(block, "sim", scatter_dimension=1, tiled=True) / (
        nfield * depth * RANK
    )
    return (state, gram_x, gram_y, core)


def solution(mesh):
    in_specs = (P(None, None, "sim", ("grp", "gz")), P(), P(), P(), P(), P())
    out_specs = (
        P(None, None, "sim", ("grp", "gz")),
        P("sim", ("grp", "gz")),
        P(("grp", "gz"), "sim"),
        P(None, None, "sim", ("grp", "gz")),
    )
    return jax.shard_map(shards, mesh=mesh, in_specs=in_specs, out_specs=out_specs, check_vma=False)
```

profile of v0, /device:TPU:8, one launch (start us, length us, event | category | flops | bytes accessed | tf_op | source)
XLA Modules:
  0.0 980.0 jit_solution(15464868327093606342)
XLA Ops:
  10.4 3.6 collective-permute-start
  15.5 3.4 collective-permute-start.3
  18.9 13.5 %collective-permute-start.2 = (f32[8,2,34,1]{3,0,2,1:T(8,128)S(1)}, f32[8,2,34,1]{3,0,2,1:T(8,128)S(1)}, u32[]{:S(2)}, u32[]{:S(2)}) collective-permute-start(f32[8,2,34,1]{3,0,2,1:T(8,128)S(1)} %get-tuple-element.31), channel_id=1, source_target_pairs={{1,0},{2,1},{3,2},{4,3},{5,4},{6,5},{7,6},{8,7},{9,8},{10,9},{11,1... | collective-permute-start | bytes 6536 | tf_op jit(solution)/shard_map/ppermute | solution.py:22
  34.1 4.8 collective-permute-done.3
  39.0 15.9 %collective-permute-done.2 = f32[8,2,34,1]{3,0,2,1:T(8,128)S(1)} collective-permute-done((f32[8,2,34,1]{3,0,2,1:T(8,128)S(1)}, f32[8,2,34,1]{3,0,2,1:T(8,128)S(1)}, u32[]{:S(2)}, u32[]{:S(2)}) %collective-permute-start.2) | collective-permute-done | bytes 2208 | tf_op jit(solution)/shard_map/ppermute | solution.py:22
  56.5 3.9 collective-permute-start.4
  67.8 10.5 %collective-permute-start.6 = (f32[8,2,34,1]{3,0,2,1:T(8,128)S(1)}, f32[8,2,34,1]{3,0,2,1:T(8,128)S(1)}, u32[]{:S(2)}, u32[]{:S(2)}) collective-permute-start(f32[8,2,34,1]{3,0,2,1:T(8,128)S(1)} %get-tuple-element.29), channel_id=1, source_target_pairs={{1,0},{2,1},{3,2},{4,3},{5,4},{6,5},{7,6},{8,7},{9,8},{10,9},{11,1... | collective-permute-start | bytes 6536 | tf_op jit(solution)/shard_map/ppermute | solution.py:22
  78.4 9.8 collective-permute-done.7
  92.7 13.1 %collective-permute-start.8 = (f32[8,2,1,64]{3,0,2,1:T(8,128)S(1)}, f32[8,2,1,64]{3,0,2,1:T(8,128)S(1)}, u32[]{:S(2)}, u32[]{:S(2)}) collective-permute-start(f32[8,2,1,64]{3,0,2,1:T(8,128)S(1)} %get-tuple-element.53), channel_id=1, source_target_pairs={{16,0},{32,16},{48,32},{64,48},{80,64},{96,80},{112,96},{128,112},... | collective-permute-start | bytes 12296 | tf_op jit(solution)/shard_map/ppermute | solution.py:22
  112.9 10.4 %collective-permute-start.10 = (f32[8,2,34,1]{3,0,2,1:T(8,128)S(1)}, f32[8,2,34,1]{3,0,2,1:T(8,128)S(1)}, u32[]{:S(2)}, u32[]{:S(2)}) collective-permute-start(f32[8,2,34,1]{3,0,2,1:T(8,128)S(1)} %get-tuple-element.27), channel_id=1, source_target_pairs={{1,0},{2,1},{3,2},{4,3},{5,4},{6,5},{7,6},{8,7},{9,8},{10,9},{11,1... | collective-permute-start | bytes 6536 | tf_op jit(solution)/shard_map/ppermute | solution.py:22
  123.3 17.0 %collective-permute-done.11 = f32[8,2,34,1]{3,0,2,1:T(8,128)S(1)} collective-permute-done((f32[8,2,34,1]{3,0,2,1:T(8,128)S(1)}, f32[8,2,34,1]{3,0,2,1:T(8,128)S(1)}, u32[]{:S(2)}, u32[]{:S(2)}) %collective-permute-start.11) | collective-permute-done | bytes 2208 | tf_op jit(solution)/shard_map/ppermute | solution.py:20
  148.0 10.2 %collective-permute-start.14 = (f32[8,2,34,1]{3,0,2,1:T(8,128)S(1)}, f32[8,2,34,1]{3,0,2,1:T(8,128)S(1)}, u32[]{:S(2)}, u32[]{:S(2)}) collective-permute-start(f32[8,2,34,1]{3,0,2,1:T(8,128)S(1)} %get-tuple-element.25), channel_id=1, source_target_pairs={{1,0},{2,1},{3,2},{4,3},{5,4},{6,5},{7,6},{8,7},{9,8},{10,9},{11,1... | collective-permute-start | bytes 6536 | tf_op jit(solution)/shard_map/ppermute | solution.py:22
  160.1 9.8 collective-permute-done.14
  169.9 16.0 %collective-permute-done.15 = f32[8,2,34,1]{3,0,2,1:T(8,128)S(1)} collective-permute-done((f32[8,2,34,1]{3,0,2,1:T(8,128)S(1)}, f32[8,2,34,1]{3,0,2,1:T(8,128)S(1)}, u32[]{:S(2)}, u32[]{:S(2)}) %collective-permute-start.15) | collective-permute-done | bytes 2208 | tf_op jit(solution)/shard_map/ppermute | solution.py:20
  195.5 9.9 %collective-permute-start.18 = (f32[8,2,34,1]{3,0,2,1:T(8,128)S(1)}, f32[8,2,34,1]{3,0,2,1:T(8,128)S(1)}, u32[]{:S(2)}, u32[]{:S(2)}) collective-permute-start(f32[8,2,34,1]{3,0,2,1:T(8,128)S(1)} %get-tuple-element.23), channel_id=1, source_target_pairs={{1,0},{2,1},{3,2},{4,3},{5,4},{6,5},{7,6},{8,7},{9,8},{10,9},{11,1... | collective-permute-start | bytes 6536 | tf_op jit(solution)/shard_map/ppermute | solution.py:22
  205.5 8.9 collective-permute-done.19
  223.8 9.9 %collective-permute-start.22 = (f32[8,2,34,1]{3,0,2,1:T(8,128)S(1)}, f32[8,2,34,1]{3,0,2,1:T(8,128)S(1)}, u32[]{:S(2)}, u32[]{:S(2)}) collective-permute-start(f32[8,2,34,1]{3,0,2,1:T(8,128)S(1)} %get-tuple-element.21), channel_id=1, source_target_pairs={{1,0},{2,1},{3,2},{4,3},{5,4},{6,5},{7,6},{8,7},{9,8},{10,9},{11,1... | collective-permute-start | bytes 6536 | tf_op jit(solution)/shard_map/ppermute | solution.py:22
  233.7 5.2 collective-permute-done.23
  245.2 3.9 collective-permute-done.25
  251.2 9.9 %collective-permute-start.26 = (f32[8,2,34,1]{3,0,2,1:T(8,128)S(1)}, f32[8,2,34,1]{3,0,2,1:T(8,128)S(1)}, u32[]{:S(2)}, u32[]{:S(2)}) collective-permute-start(f32[8,2,34,1]{3,0,2,1:T(8,128)S(1)} %get-tuple-element.19), channel_id=1, source_target_pairs={{1,0},{2,1},{3,2},{4,3},{5,4},{6,5},{7,6},{8,7},{9,8},{10,9},{11,1... | collective-permute-start | bytes 6536 | tf_op jit(solution)/shard_map/ppermute | solution.py:22
  261.2 8.2 collective-permute-done.27
  269.8 5.5 collective-permute-start.28
  280.6 7.2 collective-permute-start.30
  289.8 10.9 %collective-permute-done.30 = f32[8,2,34,1]{3,0,2,1:T(8,128)S(1)} collective-permute-done((f32[8,2,34,1]{3,0,2,1:T(8,128)S(1)}, f32[8,2,34,1]{3,0,2,1:T(8,128)S(1)}, u32[]{:S(2)}, u32[]{:S(2)}) %collective-permute-start.30) | collective-permute-done | bytes 2208 | tf_op jit(solution)/shard_map/ppermute | solution.py:22
  300.7 5.3 collective-permute-done.31
  311.3 181.6 %reduce-scatter.7.cloned.1.call-done = f32[8,2,4,64]{3,0,1,2:T(8,128)} async-done(((f32[8,2,128,64]{3,0,1,2:T(8,128)}), f32[8,2,4,64]{3,0,1,2:T(8,128)}) %reduce-scatter.7.cloned.1.call-update) | async-done | bytes 16400 | tf_op jit(solution)/shard_map/reduce_scatter | solution.py:70
  493.9 148.2 %all_gather.7 = f32[8,2,4,1024]{0,2,1,3:T(4,128)S(1)} all-gather(f32[8,2,4,64]{0,2,1,3:T(4,128)S(1)} %copy.68), channel_id=1, replica_groups=mesh['sim'=32,'grp'=4,'gz'=4] {'grp','gz'}, dimensions={3}, use_global_device_ids=true | all-gather | bytes 278528 | tf_op jit(solution)/shard_map/all_gather | solution.py:77
  642.1 7.6 fusion.4
  650.6 108.4 %all-reduce = f32[8,2,4,128]{3,0,2,1:T(8,128)S(1)} all-reduce(f32[8,2,4,128]{3,0,2,1:T(8,128)S(1)} %fusion.99), channel_id=5, replica_groups=mesh['sim'=32,'grp'=4,'gz'=4] {'grp','gz'}, use_global_device_ids=true, to_apply=%region_3.4.clone | all-reduce | flops 8192 | bytes 65536
  759.1 10.7 %fusion.7 = f32[1024,32]{1,0:T(8,128)} fusion(f32[8,2,32,64]{3,2,1,0:T(8,128)S(1)} %copy.71, f32[8,2,1024,64]{3,0,2,1:T(8,128)} %all-gather.2.cloned.1.call-done), kind=kOutput, calls=%fused_computation.5 | convolution fusion | flops 402653184 | bytes 4456448 | tf_op jit(solution)/shard_map/fzxy,fzwy->xw/dot_general | solution.py:64
  770.5 83.8 %reduce-scatter.9.cloned.1.call-done = f32[64,32]{0,1:T(8,128)} async-done(((f32[64,1024]{0,1:T(8,128)}), f32[64,32]{0,1:T(8,128)}) %reduce-scatter.9.cloned.1.call-update) | async-done | bytes 8208 | tf_op jit(solution)/shard_map/reduce_scatter | solution.py:85
  855.6 116.4 %reduce-scatter.11.cloned.1.call-done = f32[64,32]{1,0:T(8,128)} async-done(((f32[1024,32]{1,0:T(8,128)}), f32[64,32]{1,0:T(8,128)}) %reduce-scatter.11.cloned.1.call-update) | async-done | bytes 8208
  (118 shorter events, 81.5 us)
Async XLA Ops:
  7.2 485.7 %reduce-scatter.7.cloned.1.call-start = ((), (), s32[]{:S(2)}) async-start(), calls=%async_computation.4 | async-start | bytes 1081344 | tf_op jit(solution)/shard_map/reduce_scatter | solution.py:70
  8.5 5.6 collective-permute-start.1
  10.4 5.0 collective-permute-start
  15.5 23.4 %collective-permute-start.3 = (f32[8,2,34,1]{3,0,2,1:T(8,128)S(1)}, f32[8,2,34,1]{3,0,2,1:T(8,128)S(1)}, u32[]{:S(2)}, u32[]{:S(2)}) collective-permute-start(f32[8,2,34,1]{3,0,2,1:T(8,128)S(1)} %get-tuple-element.30), channel_id=1, source_target_pairs={{0,1},{1,2},{2,3},{3,4},{4,5},{5,6},{6,7},{7,8},{8,9},{9,10},{10,1... | collective-permute-start | bytes 6536 | tf_op jit(solution)/shard_map/ppermute | solution.py:20
  18.9 36.0 %collective-permute-start.2 = (f32[8,2,34,1]{3,0,2,1:T(8,128)S(1)}, f32[8,2,34,1]{3,0,2,1:T(8,128)S(1)}, u32[]{:S(2)}, u32[]{:S(2)}) collective-permute-start(f32[8,2,34,1]{3,0,2,1:T(8,128)S(1)} %get-tuple-element.31), channel_id=1, source_target_pairs={{1,0},{2,1},{3,2},{4,3},{5,4},{6,5},{7,6},{8,7},{9,8},{10,9},{11,1... | collective-permute-start | bytes 6536 | tf_op jit(solution)/shard_map/ppermute | solution.py:22
  56.5 5.8 collective-permute-start.4
  60.4 5.3 collective-permute-start.5
  65.9 22.2 %collective-permute-start.7 = (f32[8,2,34,1]{3,0,2,1:T(8,128)S(1)}, f32[8,2,34,1]{3,0,2,1:T(8,128)S(1)}, u32[]{:S(2)}, u32[]{:S(2)}) collective-permute-start(f32[8,2,34,1]{3,0,2,1:T(8,128)S(1)} %get-tuple-element.28), channel_id=1, source_target_pairs={{0,1},{1,2},{2,3},{3,4},{4,5},{5,6},{6,7},{7,8},{8,9},{9,10},{10,1... | collective-permute-start | bytes 6536 | tf_op jit(solution)/shard_map/ppermute | solution.py:20
  67.8 23.3 %collective-permute-start.6 = (f32[8,2,34,1]{3,0,2,1:T(8,128)S(1)}, f32[8,2,34,1]{3,0,2,1:T(8,128)S(1)}, u32[]{:S(2)}, u32[]{:S(2)}) collective-permute-start(f32[8,2,34,1]{3,0,2,1:T(8,128)S(1)} %get-tuple-element.29), channel_id=1, source_target_pairs={{1,0},{2,1},{3,2},{4,3},{5,4},{6,5},{7,6},{8,7},{9,8},{10,9},{11,1... | collective-permute-start | bytes 6536 | tf_op jit(solution)/shard_map/ppermute | solution.py:22
  92.7 15.1 %collective-permute-start.8 = (f32[8,2,1,64]{3,0,2,1:T(8,128)S(1)}, f32[8,2,1,64]{3,0,2,1:T(8,128)S(1)}, u32[]{:S(2)}, u32[]{:S(2)}) collective-permute-start(f32[8,2,1,64]{3,0,2,1:T(8,128)S(1)} %get-tuple-element.53), channel_id=1, source_target_pairs={{16,0},{32,16},{48,32},{64,48},{80,64},{96,80},{112,96},{128,112},... | collective-permute-start | bytes 12296 | tf_op jit(solution)/shard_map/ppermute | solution.py:22
  105.8 5.0 collective-permute-start.9
  110.9 29.4 %collective-permute-start.11 = (f32[8,2,34,1]{3,0,2,1:T(8,128)S(1)}, f32[8,2,34,1]{3,0,2,1:T(8,128)S(1)}, u32[]{:S(2)}, u32[]{:S(2)}) collective-permute-start(f32[8,2,34,1]{3,0,2,1:T(8,128)S(1)} %get-tuple-element.26), channel_id=1, source_target_pairs={{0,1},{1,2},{2,3},{3,4},{4,5},{5,6},{6,7},{7,8},{8,9},{9,10},{10,1... | collective-permute-start | bytes 6536 | tf_op jit(solution)/shard_map/ppermute | solution.py:20
  112.9 27.4 %collective-permute-start.10 = (f32[8,2,34,1]{3,0,2,1:T(8,128)S(1)}, f32[8,2,34,1]{3,0,2,1:T(8,128)S(1)}, u32[]{:S(2)}, u32[]{:S(2)}) collective-permute-start(f32[8,2,34,1]{3,0,2,1:T(8,128)S(1)} %get-tuple-element.27), channel_id=1, source_target_pairs={{1,0},{2,1},{3,2},{4,3},{5,4},{6,5},{7,6},{8,7},{9,8},{10,9},{11,1... | collective-permute-start | bytes 6536 | tf_op jit(solution)/shard_map/ppermute | solution.py:22
  142.8 5.0 collective-permute-start.13
  148.0 21.9 %collective-permute-start.14 = (f32[8,2,34,1]{3,0,2,1:T(8,128)S(1)}, f32[8,2,34,1]{3,0,2,1:T(8,128)S(1)}, u32[]{:S(2)}, u32[]{:S(2)}) collective-permute-start(f32[8,2,34,1]{3,0,2,1:T(8,128)S(1)} %get-tuple-element.25), channel_id=1, source_target_pairs={{1,0},{2,1},{3,2},{4,3},{5,4},{6,5},{7,6},{8,7},{9,8},{10,9},{11,1... | collective-permute-start | bytes 6536 | tf_op jit(solution)/shard_map/ppermute | solution.py:22
  158.2 27.7 %collective-permute-start.15 = (f32[8,2,34,1]{3,0,2,1:T(8,128)S(1)}, f32[8,2,34,1]{3,0,2,1:T(8,128)S(1)}, u32[]{:S(2)}, u32[]{:S(2)}) collective-permute-start(f32[8,2,34,1]{3,0,2,1:T(8,128)S(1)} %get-tuple-element.24), channel_id=1, source_target_pairs={{0,1},{1,2},{2,3},{3,4},{4,5},{5,6},{6,7},{7,8},{8,9},{9,10},{10,1... | collective-permute-start | bytes 6536 | tf_op jit(solution)/shard_map/ppermute | solution.py:20
  188.4 5.0 collective-permute-start.17
  193.6 20.8 %collective-permute-start.19 = (f32[8,2,34,1]{3,0,2,1:T(8,128)S(1)}, f32[8,2,34,1]{3,0,2,1:T(8,128)S(1)}, u32[]{:S(2)}, u32[]{:S(2)}) collective-permute-start(f32[8,2,34,1]{3,0,2,1:T(8,128)S(1)} %get-tuple-element.22), channel_id=1, source_target_pairs={{0,1},{1,2},{2,3},{3,4},{4,5},{5,6},{6,7},{7,8},{8,9},{9,10},{10,1... | collective-permute-start | bytes 6536 | tf_op jit(solution)/shard_map/ppermute | solution.py:20
  195.5 18.8 %collective-permute-start.18 = (f32[8,2,34,1]{3,0,2,1:T(8,128)S(1)}, f32[8,2,34,1]{3,0,2,1:T(8,128)S(1)}, u32[]{:S(2)}, u32[]{:S(2)}) collective-permute-start(f32[8,2,34,1]{3,0,2,1:T(8,128)S(1)} %get-tuple-element.23), channel_id=1, source_target_pairs={{1,0},{2,1},{3,2},{4,3},{5,4},{6,5},{7,6},{8,7},{9,8},{10,9},{11,1... | collective-permute-start | bytes 6536 | tf_op jit(solution)/shard_map/ppermute | solution.py:22
  216.7 5.0 collective-permute-start.21
  221.8 17.1 %collective-permute-start.23 = (f32[8,2,34,1]{3,0,2,1:T(8,128)S(1)}, f32[8,2,34,1]{3,0,2,1:T(8,128)S(1)}, u32[]{:S(2)}, u32[]{:S(2)}) collective-permute-start(f32[8,2,34,1]{3,0,2,1:T(8,128)S(1)} %get-tuple-element.20), channel_id=1, source_target_pairs={{0,1},{1,2},{2,3},{3,4},{4,5},{5,6},{6,7},{7,8},{8,9},{9,10},{10,1... | collective-permute-start | bytes 6536 | tf_op jit(solution)/shard_map/ppermute | solution.py:20
  223.8 16.3 %collective-permute-start.22 = (f32[8,2,34,1]{3,0,2,1:T(8,128)S(1)}, f32[8,2,34,1]{3,0,2,1:T(8,128)S(1)}, u32[]{:S(2)}, u32[]{:S(2)}) collective-permute-start(f32[8,2,34,1]{3,0,2,1:T(8,128)S(1)} %get-tuple-element.21), channel_id=1, source_target_pairs={{1,0},{2,1},{3,2},{4,3},{5,4},{6,5},{7,6},{8,7},{9,8},{10,9},{11,1... | collective-permute-start | bytes 6536 | tf_op jit(solution)/shard_map/ppermute | solution.py:22
  243.3 5.8 collective-permute-start.25
  249.3 20.1 %collective-permute-start.27 = (f32[8,2,34,1]{3,0,2,1:T(8,128)S(1)}, f32[8,2,34,1]{3,0,2,1:T(8,128)S(1)}, u32[]{:S(2)}, u32[]{:S(2)}) collective-permute-start(f32[8,2,34,1]{3,0,2,1:T(8,128)S(1)} %get-tuple-element.18), channel_id=1, source_target_pairs={{0,1},{1,2},{2,3},{3,4},{4,5},{5,6},{6,7},{7,8},{8,9},{9,10},{10,1... | collective-permute-start | bytes 6536 | tf_op jit(solution)/shard_map/ppermute | solution.py:20
  251.2 18.2 %collective-permute-start.26 = (f32[8,2,34,1]{3,0,2,1:T(8,128)S(1)}, f32[8,2,34,1]{3,0,2,1:T(8,128)S(1)}, u32[]{:S(2)}, u32[]{:S(2)}) collective-permute-start(f32[8,2,34,1]{3,0,2,1:T(8,128)S(1)} %get-tuple-element.19), channel_id=1, source_target_pairs={{1,0},{2,1},{3,2},{4,3},{5,4},{6,5},{7,6},{8,7},{9,8},{10,9},{11,1... | collective-permute-start | bytes 6536 | tf_op jit(solution)/shard_map/ppermute | solution.py:22
  269.8 7.4 collective-permute-start.28
  275.3 5.2 collective-permute-start.29
  280.6 20.0 %collective-permute-start.30 = (f32[8,2,34,1]{3,0,2,1:T(8,128)S(1)}, f32[8,2,34,1]{3,0,2,1:T(8,128)S(1)}, u32[]{:S(2)}, u32[]{:S(2)}) collective-permute-start(f32[8,2,34,1]{3,0,2,1:T(8,128)S(1)} %get-tuple-element.17), channel_id=1, source_target_pairs={{1,0},{2,1},{3,2},{4,3},{5,4},{6,5},{7,6},{8,7},{9,8},{10,9},{11,1... | collective-permute-start | bytes 6536 | tf_op jit(solution)/shard_map/ppermute | solution.py:22
  287.8 18.1 %collective-permute-start.31 = (f32[8,2,34,1]{3,0,2,1:T(8,128)S(1)}, f32[8,2,34,1]{3,0,2,1:T(8,128)S(1)}, u32[]{:S(2)}, u32[]{:S(2)}) collective-permute-start(f32[8,2,34,1]{3,0,2,1:T(8,128)S(1)} %get-tuple-element.16), channel_id=1, source_target_pairs={{0,1},{1,2},{2,3},{3,4},{4,5},{5,6},{6,7},{7,8},{8,9},{9,10},{10,1... | collective-permute-start | bytes 6536 | tf_op jit(solution)/shard_map/ppermute | solution.py:20
  308.5 450.5 %all-gather.2.cloned.1.call-start = ((), (), s32[]{:S(2)}) async-start(), calls=%async_computation.3 | async-start | bytes 8650752 | tf_op jit(solution)/shard_map/all_gather | solution.py:65
  309.3 545.0 %reduce-scatter.9.cloned.1.call-start = ((), (), s32[]{:S(2)}) async-start(), calls=%async_computation.5 | async-start | bytes 540672 | tf_op jit(solution)/shard_map/reduce_scatter | solution.py:85
  649.7 322.3 %reduce-scatter.11.cloned.1.call-start = ((), (), s32[]{:S(2)}) async-start(), calls=%async_computation.6 | async-start | bytes 557056
  (11 other events, 1338.7 us)
Sparse Core Ops, SparseCore 0:
  308.6 184.2 reduce-scatter.6
  495.3 193.5 all-gather.1
  691.9 162.3 reduce-scatter.8
  858.2 113.7 reduce-scatter.10
where the time goes:
time: 981 us; the launch traced here: 980 us
  waiting for transfers between devices  520 us (53%)
  blocking collectives  257 us (26%)
  starting transfers between devices  150 us (15%)
  matrix products  25.9 us (3%)
  between operations  15.2 us (2%)
    reduce_scatter x1, waiting for transfers between devices, shards(): lax.psum_scatter(partial_proj, 'sim', scatter_dimension=2, tiled=True)  182 us
    all_gather x1, blocking collectives, shards(): lax.all_gather(projected, ('grp', 'gz'), axis=3, tiled=True)  148 us
    unnamed x5, waiting for transfers between devices  117 us
    ppermute x16, starting transfers between devices, with_halo(): lax.ppermute(head, axis, [((i + 1) % count, i) for i in range(count)])  116 us
    unnamed x1, blocking collectives  108 us
    ppermute x16, waiting for transfers between devices, with_halo(): lax.ppermute(tail, axis, [(i, (i + 1) % count) for i in range(count)])  96.2 us
    reduce_scatter x1, waiting for transfers between devices, shards(): lax.psum_scatter(block, 'sim', scatter_dimension=1, tiled=True)  83.8 us
    ppermute x16, waiting for transfers between devices, with_halo(): lax.ppermute(head, axis, [((i + 1) % count, i) for i in range(count)])  41 us
  transfers between devices with their start and end apart: 36, of which 24 were waited for; matrix products, arithmetic and copies ran while one was open for 3% of the time, Pallas kernels for 0%

commit v1 on v0

--- a/solution.py
+++ b/solution.py
@@ -2,6 +2,7 @@
 import jax.numpy as jnp
 from jax import lax
 from jax.sharding import PartitionSpec as P
+from jax.lax import all_to_all, axis_size
 
 NY = 1024
 RANK = 128
@@ -74,7 +75,15 @@
     block = jnp.einsum(
         "fzry,fzrv->yv",
         projected,
-        lax.all_gather(projected, ("grp", "gz"), axis=3, tiled=True),
+        jnp.concatenate(
+            all_to_all(
+                jnp.stack([projected for _ in range(axis_size(("grp", "gz")))], 0),
+                ("grp", "gz"),
+                0,
+                0,
+            ),
+            3,
+        ),
         precision=highest,
     )
     own_basis_y = lax.dynamic_slice_in_dim(

time: 981 us -> 842 us (0.86)
  blocking collectives: 257 us -> 92.8 us
  starting transfers between devices: 150 us -> 164 us
  waiting for transfers between devices: 520 us -> 532 us
    all_gather x1 -> x0, blocking collectives: 148 us -> none  [shards(): lax.all_gather(projected, ('grp', 'gz'), axis=3, tiled=True)]
    unnamed x1, blocking collectives: 108 us -> 92.8 us
    all_to_all x0 -> x1, waiting for transfers between devices: none -> 13.9 us  [shards(): all_to_all(jnp.stack([projected for _ in range(axis_size(('grp', 'gz')))]...]
    all_to_all x0 -> x1, starting transfers between devices: none -> 13.4 us  [shards(): all_to_all(jnp.stack([projected for _ in range(axis_size(('grp', 'gz')))]...]
  transfers between devices with their start and end apart: 36 -> 37, of which waited for: 24 -> 25; matrix products, arithmetic and copies ran while one was open for 3% -> 3% of each run, Pallas kernels for 0% -> 0%
where the time goes in v1:
time: 842 us; the launch traced here: 840 us
  waiting for transfers between devices  532 us (63%)
  starting transfers between devices  164 us (19%)
  blocking collectives  92.8 us (11%)
  matrix products  20.8 us (2%)
  between operations  15.2 us (2%)
  local copies, waits for them, and re-layouts  11.8 us (1%)
    reduce_scatter x1, waiting for transfers between devices, shards(): lax.psum_scatter(partial_proj, 'sim', scatter_dimension=2, tiled=True)  179 us
    unnamed x5, waiting for transfers between devices  117 us
    ppermute x16, starting transfers between devices, with_halo(): lax.ppermute(head, axis, [((i + 1) % count, i) for i in range(count)])  116 us
    ppermute x16, waiting for transfers between devices, with_halo(): lax.ppermute(tail, axis, [(i, (i + 1) % count) for i in range(count)])  96.2 us
    unnamed x1, blocking collectives  92.8 us
    reduce_scatter x1, waiting for transfers between devices, shards(): lax.psum_scatter(block, 'sim', scatter_dimension=1, tiled=True)  84.7 us
    ppermute x16, waiting for transfers between devices, with_halo(): lax.ppermute(head, axis, [((i + 1) % count, i) for i in range(count)])  41 us
    ppermute x16, starting transfers between devices, with_halo(): lax.ppermute(tail, axis, [(i, (i + 1) % count) for i in range(count)])  33.7 us
  transfers between devices with their start and end apart: 37, of which 25 were waited for; matrix products, arithmetic and copies ran while one was open for 3% of the time, Pallas kernels for 0%

profile of v1, /device:TPU:8, one launch (start us, length us, event | category | flops | bytes accessed | tf_op | source)
XLA Modules:
  0.0 840.1 jit_solution(13027976921097842774)
XLA Ops:
  10.4 3.6 collective-permute-start
  15.5 3.4 collective-permute-start.3
  18.9 13.5 %collective-permute-start.2 = (f32[8,2,34,1]{3,0,2,1:T(8,128)S(1)}, f32[8,2,34,1]{3,0,2,1:T(8,128)S(1)}, u32[]{:S(2)}, u32[]{:S(2)}) collective-permute-start(f32[8,2,34,1]{3,0,2,1:T(8,128)S(1)} %get-tuple-element.27), channel_id=1, source_target_pairs={{1,0},{2,1},{3,2},{4,3},{5,4},{6,5},{7,6},{8,7},{9,8},{10,9},{11,1... | collective-permute-start | bytes 6536 | tf_op jit(solution)/shard_map/ppermute | solution.py:23
  34.1 4.8 collective-permute-done.3
  39.0 15.9 %collective-permute-done.2 = f32[8,2,34,1]{3,0,2,1:T(8,128)S(1)} collective-permute-done((f32[8,2,34,1]{3,0,2,1:T(8,128)S(1)}, f32[8,2,34,1]{3,0,2,1:T(8,128)S(1)}, u32[]{:S(2)}, u32[]{:S(2)}) %collective-permute-start.2) | collective-permute-done | bytes 2208 | tf_op jit(solution)/shard_map/ppermute | solution.py:23
  56.5 3.9 collective-permute-start.4
  67.8 10.5 %collective-permute-start.6 = (f32[8,2,34,1]{3,0,2,1:T(8,128)S(1)}, f32[8,2,34,1]{3,0,2,1:T(8,128)S(1)}, u32[]{:S(2)}, u32[]{:S(2)}) collective-permute-start(f32[8,2,34,1]{3,0,2,1:T(8,128)S(1)} %get-tuple-element.25), channel_id=1, source_target_pairs={{1,0},{2,1},{3,2},{4,3},{5,4},{6,5},{7,6},{8,7},{9,8},{10,9},{11,1... | collective-permute-start | bytes 6536 | tf_op jit(solution)/shard_map/ppermute | solution.py:23
  78.4 9.8 %collective-permute-done.7 = f32[8,2,34,1]{3,0,2,1:T(8,128)S(1)} collective-permute-done((f32[8,2,34,1]{3,0,2,1:T(8,128)S(1)}, f32[8,2,34,1]{3,0,2,1:T(8,128)S(1)}, u32[]{:S(2)}, u32[]{:S(2)}) %collective-permute-start.7) | collective-permute-done | bytes 2208 | tf_op jit(solution)/shard_map/ppermute | solution.py:21
  92.7 13.1 %collective-permute-start.8 = (f32[8,2,1,64]{3,0,2,1:T(8,128)S(1)}, f32[8,2,1,64]{3,0,2,1:T(8,128)S(1)}, u32[]{:S(2)}, u32[]{:S(2)}) collective-permute-start(f32[8,2,1,64]{3,0,2,1:T(8,128)S(1)} %get-tuple-element.49), channel_id=1, source_target_pairs={{16,0},{32,16},{48,32},{64,48},{80,64},{96,80},{112,96},{128,112},... | collective-permute-start | bytes 12296 | tf_op jit(solution)/shard_map/ppermute | solution.py:23
  112.9 10.4 %collective-permute-start.10 = (f32[8,2,34,1]{3,0,2,1:T(8,128)S(1)}, f32[8,2,34,1]{3,0,2,1:T(8,128)S(1)}, u32[]{:S(2)}, u32[]{:S(2)}) collective-permute-start(f32[8,2,34,1]{3,0,2,1:T(8,128)S(1)} %get-tuple-element.23), channel_id=1, source_target_pairs={{1,0},{2,1},{3,2},{4,3},{5,4},{6,5},{7,6},{8,7},{9,8},{10,9},{11,1... | collective-permute-start | bytes 6536 | tf_op jit(solution)/shard_map/ppermute | solution.py:23
  123.3 17.0 %collective-permute-done.11 = f32[8,2,34,1]{3,0,2,1:T(8,128)S(1)} collective-permute-done((f32[8,2,34,1]{3,0,2,1:T(8,128)S(1)}, f32[8,2,34,1]{3,0,2,1:T(8,128)S(1)}, u32[]{:S(2)}, u32[]{:S(2)}) %collective-permute-start.11) | collective-permute-done | bytes 2208 | tf_op jit(solution)/shard_map/ppermute | solution.py:21
  148.0 10.2 %collective-permute-start.14 = (f32[8,2,34,1]{3,0,2,1:T(8,128)S(1)}, f32[8,2,34,1]{3,0,2,1:T(8,128)S(1)}, u32[]{:S(2)}, u32[]{:S(2)}) collective-permute-start(f32[8,2,34,1]{3,0,2,1:T(8,128)S(1)} %get-tuple-element.21), channel_id=1, source_target_pairs={{1,0},{2,1},{3,2},{4,3},{5,4},{6,5},{7,6},{8,7},{9,8},{10,9},{11,1... | collective-permute-start | bytes 6536 | tf_op jit(solution)/shard_map/ppermute | solution.py:23
  160.1 9.8 %collective-permute-done.14 = f32[8,2,34,1]{3,0,2,1:T(8,128)S(1)} collective-permute-done((f32[8,2,34,1]{3,0,2,1:T(8,128)S(1)}, f32[8,2,34,1]{3,0,2,1:T(8,128)S(1)}, u32[]{:S(2)}, u32[]{:S(2)}) %collective-permute-start.14) | collective-permute-done | bytes 2208 | tf_op jit(solution)/shard_map/ppermute | solution.py:23
  169.9 16.0 %collective-permute-done.15 = f32[8,2,34,1]{3,0,2,1:T(8,128)S(1)} collective-permute-done((f32[8,2,34,1]{3,0,2,1:T(8,128)S(1)}, f32[8,2,34,1]{3,0,2,1:T(8,128)S(1)}, u32[]{:S(2)}, u32[]{:S(2)}) %collective-permute-start.15) | collective-permute-done | bytes 2208 | tf_op jit(solution)/shard_map/ppermute | solution.py:21
  195.5 9.9 %collective-permute-start.18 = (f32[8,2,34,1]{3,0,2,1:T(8,128)S(1)}, f32[8,2,34,1]{3,0,2,1:T(8,128)S(1)}, u32[]{:S(2)}, u32[]{:S(2)}) collective-permute-start(f32[8,2,34,1]{3,0,2,1:T(8,128)S(1)} %get-tuple-element.19), channel_id=1, source_target_pairs={{1,0},{2,1},{3,2},{4,3},{5,4},{6,5},{7,6},{8,7},{9,8},{10,9},{11,1... | collective-permute-start | bytes 6536 | tf_op jit(solution)/shard_map/ppermute | solution.py:23
  205.5 8.9 %collective-permute-done.19 = f32[8,2,34,1]{3,0,2,1:T(8,128)S(1)} collective-permute-done((f32[8,2,34,1]{3,0,2,1:T(8,128)S(1)}, f32[8,2,34,1]{3,0,2,1:T(8,128)S(1)}, u32[]{:S(2)}, u32[]{:S(2)}) %collective-permute-start.19) | collective-permute-done | bytes 2208 | tf_op jit(solution)/shard_map/ppermute | solution.py:21
  223.8 9.9 %collective-permute-start.22 = (f32[8,2,34,1]{3,0,2,1:T(8,128)S(1)}, f32[8,2,34,1]{3,0,2,1:T(8,128)S(1)}, u32[]{:S(2)}, u32[]{:S(2)}) collective-permute-start(f32[8,2,34,1]{3,0,2,1:T(8,128)S(1)} %get-tuple-element.17), channel_id=1, source_target_pairs={{1,0},{2,1},{3,2},{4,3},{5,4},{6,5},{7,6},{8,7},{9,8},{10,9},{11,1... | collective-permute-start | bytes 6536 | tf_op jit(solution)/shard_map/ppermute | solution.py:23
  233.7 5.2 collective-permute-done.23
  245.2 3.9 collective-permute-done.25
  251.2 9.9 %collective-permute-start.26 = (f32[8,2,34,1]{3,0,2,1:T(8,128)S(1)}, f32[8,2,34,1]{3,0,2,1:T(8,128)S(1)}, u32[]{:S(2)}, u32[]{:S(2)}) collective-permute-start(f32[8,2,34,1]{3,0,2,1:T(8,128)S(1)} %get-tuple-element.15), channel_id=1, source_target_pairs={{1,0},{2,1},{3,2},{4,3},{5,4},{6,5},{7,6},{8,7},{9,8},{10,9},{11,1... | collective-permute-start | bytes 6536 | tf_op jit(solution)/shard_map/ppermute | solution.py:23
  261.2 8.2 collective-permute-done.27
  269.8 5.5 collective-permute-start.28
  280.6 7.2 collective-permute-start.30
  289.8 10.9 %collective-permute-done.30 = f32[8,2,34,1]{3,0,2,1:T(8,128)S(1)} collective-permute-done((f32[8,2,34,1]{3,0,2,1:T(8,128)S(1)}, f32[8,2,34,1]{3,0,2,1:T(8,128)S(1)}, u32[]{:S(2)}, u32[]{:S(2)}) %collective-permute-start.30) | collective-permute-done | bytes 2208 | tf_op jit(solution)/shard_map/ppermute | solution.py:23
  300.7 5.3 collective-permute-done.31
  309.3 178.6 %reduce-scatter.7.cloned.1.call-done = f32[8,2,4,64]{3,0,1,2:T(8,128)} async-done(((f32[8,2,128,64]{3,0,1,2:T(8,128)}), f32[8,2,4,64]{3,0,1,2:T(8,128)}) %reduce-scatter.7.cloned.1.call-update) | async-done | bytes 16400 | tf_op jit(solution)/shard_map/reduce_scatter | solution.py:71
  489.7 13.4 %all-to-all-start = ((f32[16,1,4096]{2,1,0:T(1,128)}), f32[16,1,4096]{2,1,0:T(1,128)S(1)}, u32[]{:S(2)}, u32[]{:S(2)}) async-start(f32[16,1,4096]{2,1,0:T(1,128)} %reshape.35), calls=%async_computation.1 | async-start | bytes 524288 | tf_op jit(solution)/shard_map/all_to_all | solution.py:79
  505.3 13.9 %all-to-all-done = f32[16,1,4096]{2,1,0:T(1,128)S(1)} async-done(((f32[16,1,4096]{2,1,0:T(1,128)}), f32[16,1,4096]{2,1,0:T(1,128)S(1)}, u32[]{:S(2)}, u32[]{:S(2)}) %all-to-all-start) | async-done | bytes 262176 | tf_op jit(solution)/shard_map/all_to_all | solution.py:79
  525.2 92.8 %all-reduce = f32[8,2,4,128]{3,0,2,1:T(8,128)S(1)} all-reduce(f32[8,2,4,128]{3,0,2,1:T(8,128)S(1)} %fusion.94), channel_id=5, replica_groups=mesh['sim'=32,'grp'=4,'gz'=4] {'grp','gz'}, use_global_device_ids=true, to_apply=%region_3.4.clone | all-reduce | flops 8192 | bytes 65536
  618.0 10.7 %fusion.2 = f32[1024,32]{1,0:T(8,128)} fusion(f32[8,2,32,64]{3,2,1,0:T(8,128)S(1)} %copy.50, f32[8,2,1024,64]{3,0,2,1:T(8,128)} %all-gather.2.cloned.1.call-done), kind=kOutput, calls=%fused_computation.2 | convolution fusion | flops 402653184 | bytes 4456448 | tf_op jit(solution)/shard_map/fzxy,fzwy->xw/dot_general | solution.py:65
  629.5 84.7 %reduce-scatter.9.cloned.1.call-done = f32[64,32]{0,1:T(8,128)} async-done(((f32[64,1024]{0,1:T(8,128)}), f32[64,32]{0,1:T(8,128)}) %reduce-scatter.9.cloned.1.call-update) | async-done | bytes 8208 | tf_op jit(solution)/shard_map/reduce_scatter | solution.py:94
  715.5 116.6 %reduce-scatter.11.cloned.1.call-done = f32[64,32]{1,0:T(8,128)} async-done(((f32[1024,32]{1,0:T(8,128)}), f32[64,32]{1,0:T(8,128)}) %reduce-scatter.11.cloned.1.call-update) | async-done | bytes 8208
  (124 shorter events, 87.6 us)
Async XLA Ops:
  7.2 480.7 %reduce-scatter.7.cloned.1.call-start = ((), (), s32[]{:S(2)}) async-start(), calls=%async_computation.5 | async-start | bytes 1081344 | tf_op jit(solution)/shard_map/reduce_scatter | solution.py:71
  8.5 5.6 collective-permute-start.1
  10.4 5.0 collective-permute-start
  15.5 23.4 %collective-permute-start.3 = (f32[8,2,34,1]{3,0,2,1:T(8,128)S(1)}, f32[8,2,34,1]{3,0,2,1:T(8,128)S(1)}, u32[]{:S(2)}, u32[]{:S(2)}) collective-permute-start(f32[8,2,34,1]{3,0,2,1:T(8,128)S(1)} %get-tuple-element.26), channel_id=1, source_target_pairs={{0,1},{1,2},{2,3},{3,4},{4,5},{5,6},{6,7},{7,8},{8,9},{9,10},{10,1... | collective-permute-start | bytes 6536 | tf_op jit(solution)/shard_map/ppermute | solution.py:21
  18.9 36.0 %collective-permute-start.2 = (f32[8,2,34,1]{3,0,2,1:T(8,128)S(1)}, f32[8,2,34,1]{3,0,2,1:T(8,128)S(1)}, u32[]{:S(2)}, u32[]{:S(2)}) collective-permute-start(f32[8,2,34,1]{3,0,2,1:T(8,128)S(1)} %get-tuple-element.27), channel_id=1, source_target_pairs={{1,0},{2,1},{3,2},{4,3},{5,4},{6,5},{7,6},{8,7},{9,8},{10,9},{11,1... | collective-permute-start | bytes 6536 | tf_op jit(solution)/shard_map/ppermute | solution.py:23
  56.5 5.8 collective-permute-start.4
  60.4 5.3 collective-permute-start.5
  65.9 22.2 %collective-permute-start.7 = (f32[8,2,34,1]{3,0,2,1:T(8,128)S(1)}, f32[8,2,34,1]{3,0,2,1:T(8,128)S(1)}, u32[]{:S(2)}, u32[]{:S(2)}) collective-permute-start(f32[8,2,34,1]{3,0,2,1:T(8,128)S(1)} %get-tuple-element.24), channel_id=1, source_target_pairs={{0,1},{1,2},{2,3},{3,4},{4,5},{5,6},{6,7},{7,8},{8,9},{9,10},{10,1... | collective-permute-start | bytes 6536 | tf_op jit(solution)/shard_map/ppermute | solution.py:21
  67.8 23.3 %collective-permute-start.6 = (f32[8,2,34,1]{3,0,2,1:T(8,128)S(1)}, f32[8,2,34,1]{3,0,2,1:T(8,128)S(1)}, u32[]{:S(2)}, u32[]{:S(2)}) collective-permute-start(f32[8,2,34,1]{3,0,2,1:T(8,128)S(1)} %get-tuple-element.25), channel_id=1, source_target_pairs={{1,0},{2,1},{3,2},{4,3},{5,4},{6,5},{7,6},{8,7},{9,8},{10,9},{11,1... | collective-permute-start | bytes 6536 | tf_op jit(solution)/shard_map/ppermute | solution.py:23
  92.7 15.1 %collective-permute-start.8 = (f32[8,2,1,64]{3,0,2,1:T(8,128)S(1)}, f32[8,2,1,64]{3,0,2,1:T(8,128)S(1)}, u32[]{:S(2)}, u32[]{:S(2)}) collective-permute-start(f32[8,2,1,64]{3,0,2,1:T(8,128)S(1)} %get-tuple-element.49), channel_id=1, source_target_pairs={{16,0},{32,16},{48,32},{64,48},{80,64},{96,80},{112,96},{128,112},... | collective-permute-start | bytes 12296 | tf_op jit(solution)/shard_map/ppermute | solution.py:23
  105.8 5.0 collective-permute-start.9
  110.9 29.4 %collective-permute-start.11 = (f32[8,2,34,1]{3,0,2,1:T(8,128)S(1)}, f32[8,2,34,1]{3,0,2,1:T(8,128)S(1)}, u32[]{:S(2)}, u32[]{:S(2)}) collective-permute-start(f32[8,2,34,1]{3,0,2,1:T(8,128)S(1)} %get-tuple-element.22), channel_id=1, source_target_pairs={{0,1},{1,2},{2,3},{3,4},{4,5},{5,6},{6,7},{7,8},{8,9},{9,10},{10,1... | collective-permute-start | bytes 6536 | tf_op jit(solution)/shard_map/ppermute | solution.py:21
  112.9 27.4 %collective-permute-start.10 = (f32[8,2,34,1]{3,0,2,1:T(8,128)S(1)}, f32[8,2,34,1]{3,0,2,1:T(8,128)S(1)}, u32[]{:S(2)}, u32[]{:S(2)}) collective-permute-start(f32[8,2,34,1]{3,0,2,1:T(8,128)S(1)} %get-tuple-element.23), channel_id=1, source_target_pairs={{1,0},{2,1},{3,2},{4,3},{5,4},{6,5},{7,6},{8,7},{9,8},{10,9},{11,1... | collective-permute-start | bytes 6536 | tf_op jit(solution)/shard_map/ppermute | solution.py:23
  142.8 5.0 collective-permute-start.13
  148.0 21.9 %collective-permute-start.14 = (f32[8,2,34,1]{3,0,2,1:T(8,128)S(1)}, f32[8,2,34,1]{3,0,2,1:T(8,128)S(1)}, u32[]{:S(2)}, u32[]{:S(2)}) collective-permute-start(f32[8,2,34,1]{3,0,2,1:T(8,128)S(1)} %get-tuple-element.21), channel_id=1, source_target_pairs={{1,0},{2,1},{3,2},{4,3},{5,4},{6,5},{7,6},{8,7},{9,8},{10,9},{11,1... | collective-permute-start | bytes 6536 | tf_op jit(solution)/shard_map/ppermute | solution.py:23
  158.2 27.7 %collective-permute-start.15 = (f32[8,2,34,1]{3,0,2,1:T(8,128)S(1)}, f32[8,2,34,1]{3,0,2,1:T(8,128)S(1)}, u32[]{:S(2)}, u32[]{:S(2)}) collective-permute-start(f32[8,2,34,1]{3,0,2,1:T(8,128)S(1)} %get-tuple-element.20), channel_id=1, source_target_pairs={{0,1},{1,2},{2,3},{3,4},{4,5},{5,6},{6,7},{7,8},{8,9},{9,10},{10,1... | collective-permute-start | bytes 6536 | tf_op jit(solution)/shard_map/ppermute | solution.py:21
  188.4 5.0 collective-permute-start.17
  193.6 20.8 %collective-permute-start.19 = (f32[8,2,34,1]{3,0,2,1:T(8,128)S(1)}, f32[8,2,34,1]{3,0,2,1:T(8,128)S(1)}, u32[]{:S(2)}, u32[]{:S(2)}) collective-permute-start(f32[8,2,34,1]{3,0,2,1:T(8,128)S(1)} %get-tuple-element.18), channel_id=1, source_target_pairs={{0,1},{1,2},{2,3},{3,4},{4,5},{5,6},{6,7},{7,8},{8,9},{9,10},{10,1... | collective-permute-start | bytes 6536 | tf_op jit(solution)/shard_map/ppermute | solution.py:21
  195.5 18.8 %collective-permute-start.18 = (f32[8,2,34,1]{3,0,2,1:T(8,128)S(1)}, f32[8,2,34,1]{3,0,2,1:T(8,128)S(1)}, u32[]{:S(2)}, u32[]{:S(2)}) collective-permute-start(f32[8,2,34,1]{3,0,2,1:T(8,128)S(1)} %get-tuple-element.19), channel_id=1, source_target_pairs={{1,0},{2,1},{3,2},{4,3},{5,4},{6,5},{7,6},{8,7},{9,8},{10,9},{11,1... | collective-permute-start | bytes 6536 | tf_op jit(solution)/shard_map/ppermute | solution.py:23
  221.8 17.1 %collective-permute-start.23 = (f32[8,2,34,1]{3,0,2,1:T(8,128)S(1)}, f32[8,2,34,1]{3,0,2,1:T(8,128)S(1)}, u32[]{:S(2)}, u32[]{:S(2)}) collective-permute-start(f32[8,2,34,1]{3,0,2,1:T(8,128)S(1)} %get-tuple-element.16), channel_id=1, source_target_pairs={{0,1},{1,2},{2,3},{3,4},{4,5},{5,6},{6,7},{7,8},{8,9},{9,10},{10,1... | collective-permute-start | bytes 6536 | tf_op jit(solution)/shard_map/ppermute | solution.py:21
  223.8 16.3 %collective-permute-start.22 = (f32[8,2,34,1]{3,0,2,1:T(8,128)S(1)}, f32[8,2,34,1]{3,0,2,1:T(8,128)S(1)}, u32[]{:S(2)}, u32[]{:S(2)}) collective-permute-start(f32[8,2,34,1]{3,0,2,1:T(8,128)S(1)} %get-tuple-element.17), channel_id=1, source_target_pairs={{1,0},{2,1},{3,2},{4,3},{5,4},{6,5},{7,6},{8,7},{9,8},{10,9},{11,1... | collective-permute-start | bytes 6536 | tf_op jit(solution)/shard_map/ppermute | solution.py:23
  243.3 5.8 collective-permute-start.25
  249.3 20.1 %collective-permute-start.27 = (f32[8,2,34,1]{3,0,2,1:T(8,128)S(1)}, f32[8,2,34,1]{3,0,2,1:T(8,128)S(1)}, u32[]{:S(2)}, u32[]{:S(2)}) collective-permute-start(f32[8,2,34,1]{3,0,2,1:T(8,128)S(1)} %get-tuple-element.14), channel_id=1, source_target_pairs={{0,1},{1,2},{2,3},{3,4},{4,5},{5,6},{6,7},{7,8},{8,9},{9,10},{10,1... | collective-permute-start | bytes 6536 | tf_op jit(solution)/shard_map/ppermute | solution.py:21
  251.2 18.2 %collective-permute-start.26 = (f32[8,2,34,1]{3,0,2,1:T(8,128)S(1)}, f32[8,2,34,1]{3,0,2,1:T(8,128)S(1)}, u32[]{:S(2)}, u32[]{:S(2)}) collective-permute-start(f32[8,2,34,1]{3,0,2,1:T(8,128)S(1)} %get-tuple-element.15), channel_id=1, source_target_pairs={{1,0},{2,1},{3,2},{4,3},{5,4},{6,5},{7,6},{8,7},{9,8},{10,9},{11,1... | collective-permute-start | bytes 6536 | tf_op jit(solution)/shard_map/ppermute | solution.py:23
  269.8 7.4 collective-permute-start.28
  275.3 5.2 collective-permute-start.29
  280.6 20.0 %collective-permute-start.30 = (f32[8,2,34,1]{3,0,2,1:T(8,128)S(1)}, f32[8,2,34,1]{3,0,2,1:T(8,128)S(1)}, u32[]{:S(2)}, u32[]{:S(2)}) collective-permute-start(f32[8,2,34,1]{3,0,2,1:T(8,128)S(1)} %get-tuple-element.13), channel_id=1, source_target_pairs={{1,0},{2,1},{3,2},{4,3},{5,4},{6,5},{7,6},{8,7},{9,8},{10,9},{11,1... | collective-permute-start | bytes 6536 | tf_op jit(solution)/shard_map/ppermute | solution.py:23
  287.8 18.1 %collective-permute-start.31 = (f32[8,2,34,1]{3,0,2,1:T(8,128)S(1)}, f32[8,2,34,1]{3,0,2,1:T(8,128)S(1)}, u32[]{:S(2)}, u32[]{:S(2)}) collective-permute-start(f32[8,2,34,1]{3,0,2,1:T(8,128)S(1)} %get-tuple-element.12), channel_id=1, source_target_pairs={{0,1},{1,2},{2,3},{3,4},{4,5},{5,6},{6,7},{7,8},{8,9},{9,10},{10,1... | collective-permute-start | bytes 6536 | tf_op jit(solution)/shard_map/ppermute | solution.py:21
  308.5 309.5 %all-gather.2.cloned.1.call-start = ((), (), s32[]{:S(2)}) async-start(), calls=%async_computation.4 | async-start | bytes 8650752 | tf_op jit(solution)/shard_map/all_gather | solution.py:66
  489.7 29.4 %all-to-all-start = ((f32[16,1,4096]{2,1,0:T(1,128)}), f32[16,1,4096]{2,1,0:T(1,128)S(1)}, u32[]{:S(2)}, u32[]{:S(2)}) async-start(f32[16,1,4096]{2,1,0:T(1,128)} %reshape.35), calls=%async_computation.1 | async-start | bytes 524288 | tf_op jit(solution)/shard_map/all_to_all | solution.py:79
  503.1 211.1 %reduce-scatter.9.cloned.1.call-start = ((), (), s32[]{:S(2)}) async-start(), calls=%async_computation.6 | async-start | bytes 540672 | tf_op jit(solution)/shard_map/reduce_scatter | solution.py:94
  524.3 307.9 %reduce-scatter.11.cloned.1.call-start = ((), (), s32[]{:S(2)}) async-start(), calls=%async_computation.7 | async-start | bytes 557056
  (11 other events, 1045.8 us)
Sparse Core Ops, SparseCore 0:
  308.6 179.2 reduce-scatter.6
  490.3 77.9 all-gather.1
  571.3 142.8 reduce-scatter.8
  718.1 113.9 reduce-scatter.10
